TPU v7x, 32 devices: a whole 2x2x4 slice. The times are simulated.
32 devices in a mesh: dp: 8 (over z, core), pos: 4 (over y, x).
Axes of the slice: x: 2, y: 2, z: 4, core: 2. Of those that a mesh axis runs over, the one named last changes fastest.
Arguments:
- features: bfloat16 [64, 128, 224], P(('dp', 'pos')), may hold values from -6 to 6
- counts: int32 [32], P(('dp', 'pos')), may hold values from 1 to 2, as said below
- channel_order: int32 [224], replicated, may hold values from 0 to 223, each once
Outputs:
- mean: float32 [128, 100], P('pos')
- covariance: float32 [128, 100, 100], P('pos')
Inputs may be any that keep to these rules, and one draw needn't show every extreme that they name: `counts`: some device has all 2 slots live and some device only one.
All inputs are finite; a program needn't handle non-finite values.
Results may differ from a plain program's by a relative error of at most 0.0003.
Values may be sent and summed in bfloat16 or wider, within the bound.
No kernel may reach another device: no remote copies, remote signals or barrier semaphores. Data moves between devices by JAX's collectives and lax.ppermute only.
A program may use at most 128 MiB of HBM per device.

v0:
```python
import jax
import jax.numpy as jnp
from jax import lax
from jax.sharding import PartitionSpec as P

CH = 100


def local_stats(received, source_counts, slots, rows, width):
    sources = source_counts.shape[0]
    samples = received.reshape(sources * slots, rows, width).astype(jnp.float32)
    live_mask = (jnp.arange(slots, dtype=jnp.float32)[None, :] < source_counts[:, None]).astype(
        jnp.float32
    )
    live_mask = live_mask.reshape(sources * slots)
    group_count = jnp.sum(source_counts).reshape(1)
    group_sums = jnp.sum(samples, axis=0)
    group_mean = group_sums / group_count
    centered = (samples - group_mean[None]) * live_mask[:, None, None]
    products = jnp.einsum("gpc,gpd->pcd", centered, centered, precision=lax.Precision.HIGHEST)
    return (group_count, group_sums, group_mean, products)


def common_mean(group_count, group_sums, group_mean):
    total_count, total_sums = lax.psum((group_count, group_sums), "dp")
    mean = total_sums / total_count
    offset = group_mean - mean
    weighted = offset * group_count
    return (total_count, mean, offset, weighted)


def on_device(features, counts, channel_order):
    slots, positions, channels = features.shape
    groups = lax.axis_size("pos")
    pos_dev = positions // groups
    kept = channel_order[:CH]
    picker = (kept[None, :] == jnp.arange(channels, dtype=jnp.int32)[:, None]).astype(jnp.bfloat16)
    owned = counts[0]
    slot_live = (jnp.arange(slots, dtype=jnp.int32) < owned).astype(jnp.bfloat16)
    embed = jnp.dot(
        features.reshape(slots * positions, channels), picker, preferred_element_type=jnp.float32
    )
    embed = embed.astype(jnp.bfloat16).reshape(slots, positions, CH) * slot_live[:, None, None]
    identity = jnp.eye(CH, dtype=jnp.float32)
    packed = embed.reshape(slots, groups, pos_dev * CH)
    owned_wire = jnp.broadcast_to(owned.astype(jnp.bfloat16).reshape(1, 1, 1), (1, groups, 1))
    received, source_counts = (
        lax.all_to_all(packed, "pos", split_axis=1, concat_axis=0, tiled=True),
        lax.all_to_all(owned_wire, "pos", split_axis=1, concat_axis=0, tiled=True),
    )
    source_counts = source_counts.reshape(groups).astype(jnp.float32)
    group_count, group_sums, group_mean, products = local_stats(
        received, source_counts, slots, pos_dev, CH
    )
    total_count, mean, offset, weighted = common_mean(group_count, group_sums, group_mean)
    own_term = products + offset[:, :, None] * weighted[:, None, :]
    summed = lax.psum(own_term, "dp")
    covariance = summed / (total_count[0] - 1.0) + 0.01 * identity
    return (mean, covariance)


def solution(mesh):
    in_specs = (P(("dp", "pos"), None, None), P(("dp", "pos")), P())
    out_specs = (P("pos", None), P("pos", None, None))
    return jax.shard_map(
        on_device, mesh=mesh, in_specs=in_specs, out_specs=out_specs, check_vma=False
    )
```

profile of v0, /device:TPU:0, one launch (start us, length us, event | category | flops | bytes accessed | tf_op | source)
XLA Modules:
  0.0 129.7 jit_solution(13337276662901932767)
XLA Ops:
  7.9 0.6 broadcast_in_dim.2
  8.4 5.2 %all-to-all-start.1 = ((bf16[1,4,1]{2,0,1:T(2,128)(2,1)}), bf16[1,4,1]{2,0,1:T(2,128)(2,1)S(1)}, u32[]{:S(2)}, u32[]{:S(2)}) async-start(bf16[1,4,1]{2,0,1:T(2,128)(2,1)} %broadcast_in_dim.2), calls=%async_computation.1 | async-start | bytes 4096 | tf_op jit(solution)/shard_map/all_to_all | solution.py:49
  13.6 0.7 slice.3
  14.3 0.2 fusion
  14.5 0.1 copy.19
  14.6 0.2 reshape.81
  14.8 0.1 broadcast_multiply_fusion
  14.9 0.7 copy.20
  15.6 2.6 %all-to-all-done.1 = bf16[1,4,1]{2,0,1:T(2,128)(2,1)S(1)} async-done(((bf16[1,4,1]{2,0,1:T(2,128)(2,1)}), bf16[1,4,1]{2,0,1:T(2,128)(2,1)S(1)}, u32[]{:S(2)}, u32[]{:S(2)}) %all-to-all-start.1) | async-done | bytes 40 | tf_op jit(solution)/shard_map/all_to_all | solution.py:49
  18.2 3.3 %all-to-all-start = ((bf16[2,4,3200]{2,0,1:T(2,128)(2,1)}), bf16[2,4,3200]{2,0,1:T(2,128)(2,1)S(1)}, u32[]{:S(2)}, u32[]{:S(2)}) async-start(bf16[2,4,3200]{2,0,1:T(2,128)(2,1)} %copy.20), calls=%async_computation | async-start | bytes 102400 | tf_op jit(solution)/shard_map/all_to_all | solution.py:48
  21.5 0.7 convert_reduce_fusion.1
  22.2 0.1 fusion.6
  22.3 0.1 reshape.85
  22.4 3.9 %all-to-all-done = bf16[2,4,3200]{2,0,1:T(2,128)(2,1)S(1)} async-done(((bf16[2,4,3200]{2,0,1:T(2,128)(2,1)}), bf16[2,4,3200]{2,0,1:T(2,128)(2,1)S(1)}, u32[]{:S(2)}, u32[]{:S(2)}) %all-to-all-start) | async-done | bytes 51232 | tf_op jit(solution)/shard_map/all_to_all | solution.py:48
  26.2 0.1 convert_reduce_fusion
  26.3 0.1 reduce_sum.21
  26.5 0.3 reshape.84
  26.7 27.4 %all-reduce = (f32[32,100]{1,0:T(8,128)S(1)}, f32[]{:T(128)}) all-reduce(f32[32,100]{1,0:T(8,128)S(1)} %reduce_sum.21, f32[]{:T(128)} %get-tuple-element.11), channel_id=1, replica_groups=mesh['dp'=8,'pos'=4] {'dp'}, use_global_device_ids=true, to_apply=%region_1.0 | all-reduce | flops 3201 | bytes 25608 | tf_op jit(solution)/shard_map/psum | solution.py:25
  54.2 1.9 %broadcast_multiply_fusion.1 = (f32[32,100]{1,0:T(8,128)S(1)}, f32[32,100]{1,0:T(8,128)S(1)}, f32[32,100]{1,0:T(8,128)S(1)}, f32[32,100]{1,0:T(8,128)}) fusion(f32[]{:T(128)} %get-tuple-element.11, f32[32,100]{1,0:T(8,128)S(1)} %reduce_sum.21, f32[32,100]{1,0:T(8,128)S(1)} %get-tuple-element.12, f32[]{:T(128)} %get-tuple-element.13), kind=kLoop, calls=%fused_computation.15 | loop fusion | flops 12800 | bytes 76808 | tf_op jit(solution)/shard_map/mul | solution.py:28
  56.1 0.1 subtract_multiply_fusion
  56.2 4.4 %multiply_add_fusion = f32[32,100,100]{2,1,0:T(8,128)} fusion(f32[32,100]{1,0:T(8,128)S(1)} %get-tuple-element.14, f32[32,100]{1,0:T(8,128)S(1)} %get-tuple-element.15, f32[8,32,100]{2,1,0:T(8,128)S(1)} %subtract_multiply_fusion), kind=kOutput, calls=%fused_computation.1 | convolution fusion | flops 31360000 | bytes 1408000 | tf_op jit(solution)/shard_map/gpc,gpd->pcd/dot_general | solution.py:20
  61.3 58.5 %all-reduce.3.cloned.1.call-done = f32[32,100,100]{2,1,0:T(8,128)} async-done(((f32[32,100,100]{2,1,0:T(8,128)}), f32[32,100,100]{2,1,0:T(8,128)}) %all-reduce.3.cloned.1.call-update) | async-done | bytes 1280016 | tf_op jit(solution)/shard_map/psum | solution.py:57
  119.8 1.6 %divide_add_fusion = f32[32,100,100]{2,1,0:T(8,128)S(1)} fusion(f32[32,100,100]{2,1,0:T(8,128)} %all-reduce.3.cloned.1.call-done, f32[100,100]{1,0:T(8,128)S(1)} %fusion.5, f32[]{:T(128)S(6)} %sub.17), kind=kLoop, calls=%fused_computation | loop fusion | flops 640000 | bytes 2600004 | tf_op jit(solution)/shard_map/add | solution.py:58
  121.4 1.5 %copy.23 = f32[32,100,100]{2,0,1:T(8,128)} copy(f32[32,100,100]{2,1,0:T(8,128)S(1)} %divide_add_fusion) | data formatting | bytes 2560000
  (7 shorter events, 0.1 us)
Async XLA Ops:
  7.2 7.1 %copy-start = (bf16[2,128,224]{1,2,0:T(8,128)(2,1)S(1)}, bf16[2,128,224]{1,2,0:T(8,128)(2,1)}, u32[]{:S(2)}) copy-start(bf16[2,128,224]{1,2,0:T(8,128)(2,1)} %param.3) | copy-start | bytes 344068
  8.4 9.7 %all-to-all-start.1 = ((bf16[1,4,1]{2,0,1:T(2,128)(2,1)}), bf16[1,4,1]{2,0,1:T(2,128)(2,1)S(1)}, u32[]{:S(2)}, u32[]{:S(2)}) async-start(bf16[1,4,1]{2,0,1:T(2,128)(2,1)} %broadcast_in_dim.2), calls=%async_computation.1 | async-start | bytes 4096 | tf_op jit(solution)/shard_map/all_to_all | solution.py:49
  18.2 8.1 %all-to-all-start = ((bf16[2,4,3200]{2,0,1:T(2,128)(2,1)}), bf16[2,4,3200]{2,0,1:T(2,128)(2,1)S(1)}, u32[]{:S(2)}, u32[]{:S(2)}) async-start(bf16[2,4,3200]{2,0,1:T(2,128)(2,1)} %copy.20), calls=%async_computation | async-start | bytes 102400 | tf_op jit(solution)/shard_map/all_to_all | solution.py:48
  21.5 98.3 %all-reduce.3.cloned.1.call-start = ((), (), s32[]{:S(2)}) async-start(), calls=%async_computation.2 | async-start | bytes 3407872 | tf_op jit(solution)/shard_map/psum | solution.py:57
Sparse Core Ops, SparseCore 0:
  60.7 59.0 all-reduce.2
where the time goes:
time: 130 us
  waiting for transfers between devices  65 us (50%)
  blocking collectives  27.4 us (21%)
  between operations  15.4 us (12%)
  starting transfers between devices  8.48 us (7%)
  other arithmetic  4.59 us (4%)
  matrix products  4.57 us (4%)
  local copies, waits for them, and re-layouts  4.13 us (3%)
    psum x1, waiting for transfers between devices, on_device(): summed = lax.psum(own_term, 'dp')  58.5 us
    psum x1, blocking collectives, common_mean(): total_count, total_sums = lax.psum((group_count, group_sums), 'dp')  27.4 us
    all_to_all x1, starting transfers between devices, on_device(): lax.all_to_all(owned_wire, 'pos', split_axis=1, concat_axis=0, tiled=True)  5.16 us
    dot_general x1, matrix products, local_stats(): jnp.einsum('gpc,gpd->pcd', centered, centered, precision=lax.Precision.HI...  4.36 us
    all_to_all x1, waiting for transfers between devices, on_device(): lax.all_to_all(packed, 'pos', split_axis=1, concat_axis=0, tiled=True)  3.88 us
    all_to_all x1, starting transfers between devices, on_device(): lax.all_to_all(packed, 'pos', split_axis=1, concat_axis=0, tiled=True)  3.28 us
    all_to_all x1, waiting for transfers between devices, on_device(): lax.all_to_all(owned_wire, 'pos', split_axis=1, concat_axis=0, tiled=True)  2.61 us
  transfers between devices with their start and end apart: 3, of which 3 were waited for; matrix products, arithmetic and copies ran while one was open for 2% of the time, Pallas kernels for 0%

commit v1 on v0

--- a/solution.py
+++ b/solution.py
@@ -4,6 +4,22 @@
 from jax.sharding import PartitionSpec as P
 
 CH = 100
+
+
+def exchange_in_pairs(shard, axis, split, join):
+    ways, here = (lax.axis_size(axis), lax.axis_index(axis))
+    width = shard.shape[split] // ways
+    dims = list(shard.shape)
+    dims[split] = width
+    height = dims[join]
+    dims[join] = height * ways
+    full = jnp.zeros(dims, shard.dtype)
+    for mask in range(ways):
+        part = lax.dynamic_slice_in_dim(shard, (here ^ mask) * width, width, axis=split)
+        if mask:
+            part = lax.ppermute(part, axis, [(d, d ^ mask) for d in range(ways)])
+        full = lax.dynamic_update_slice_in_dim(full, part, (here ^ mask) * height, axis=join)
+    return full
 
 
 def local_stats(received, source_counts, slots, rows, width):
@@ -46,7 +62,7 @@
     owned_wire = jnp.broadcast_to(owned.astype(jnp.bfloat16).reshape(1, 1, 1), (1, groups, 1))
     received, source_counts = (
         lax.all_to_all(packed, "pos", split_axis=1, concat_axis=0, tiled=True),
-        lax.all_to_all(owned_wire, "pos", split_axis=1, concat_axis=0, tiled=True),
+        exchange_in_pairs(owned_wire, "pos", 1, 0),
     )
     source_counts = source_counts.reshape(groups).astype(jnp.float32)
     group_count, group_sums, group_mean, products = local_stats(

time: 130 us -> 131 us (level)
  waiting for transfers between devices: 65 us -> 60.7 us
  starting transfers between devices: 8.48 us -> 12.6 us
  local copies, waits for them, and re-layouts: 4.13 us -> 5.84 us
    ppermute x0 -> x3, starting transfers between devices: none -> 8.42 us  [exchange_in_pairs(): part = lax.ppermute(part, axis, [(d, d ^ mask) for d in range(ways)])]
    all_to_all x1 -> x0, starting transfers between devices: 5.16 us -> none  [on_device(): lax.all_to_all(owned_wire, 'pos', split_axis=1, concat_axis=0, tiled=True)]
    all_to_all x1 -> x0, waiting for transfers between devices: 2.61 us -> none  [on_device(): lax.all_to_all(owned_wire, 'pos', split_axis=1, concat_axis=0, tiled=True)]
    dynamic_update_slice x0 -> x4, local copies, waits for them, and re-layouts: none -> 2.29 us  [exchange_in_pairs(): lax.dynamic_update_slice_in_dim(full, part, (here ^ mask) * height, axis=...]
    all_to_all x1, waiting for transfers between devices: 3.88 us -> 1.66 us  [on_device(): lax.all_to_all(packed, 'pos', split_axis=1, concat_axis=0, tiled=True)]
  transfers between devices with their start and end apart: 3 -> 5, of which waited for: 3 -> 2; matrix products, arithmetic and copies ran while one was open for 2% -> 4% of each run, Pallas kernels for 0% -> 0%
where the time goes in v1:
time: 131 us
  waiting for transfers between devices  60.7 us (46%)
  blocking collectives  27.2 us (21%)
  between operations  15.4 us (12%)
  starting transfers between devices  12.6 us (10%)
  local copies, waits for them, and re-layouts  5.84 us (4%)
  other arithmetic  4.6 us (4%)
  matrix products  4.57 us (3%)
    psum x1, waiting for transfers between devices, on_device(): summed = lax.psum(own_term, 'dp')  59 us
    psum x1, blocking collectives, common_mean(): total_count, total_sums = lax.psum((group_count, group_sums), 'dp')  27.2 us
    ppermute x3, starting transfers between devices, exchange_in_pairs(): part = lax.ppermute(part, axis, [(d, d ^ mask) for d in range(ways)])  8.42 us
    dot_general x1, matrix products, local_stats(): jnp.einsum('gpc,gpd->pcd', centered, centered, precision=lax.Precision.HI...  4.36 us
    all_to_all x1, starting transfers between devices, on_device(): lax.all_to_all(packed, 'pos', split_axis=1, concat_axis=0, tiled=True)  4.19 us
  transfers between devices with their start and end apart: 5, of which 2 were waited for; matrix products, arithmetic and copies ran while one was open for 4% of the time, Pallas kernels for 0%

profile of v1, /device:TPU:0, one launch (start us, length us, event | category | flops | bytes accessed | tf_op | source)
XLA Modules:
  0.0 130.9 jit_solution(3209055383485276755)
XLA Ops:
  7.9 4.3 %collective-permute-start = (bf16[1,1,1]{2,1,0:T(2,128)(2,1)}, bf16[1,1,1]{2,1,0:T(2,128)(2,1)}, u32[]{:S(2)}, u32[]{:S(2)}) collective-permute-start(bf16[1,1,1]{2,1,0:T(2,128)(2,1)} %bitcast.3), channel_id=1, source_target_pairs={{0,1},{1,0},{2,3},{3,2},{4,5},{5,4},{6,7},{7,6},{8,9},{9,8},{10,11... | collective-permute-start | bytes 14 | tf_op jit(solution)/shard_map/ppermute | solution.py:20
  12.2 2.8 %collective-permute-start.1 = (bf16[1,1,1]{2,1,0:T(2,128)(2,1)}, bf16[1,1,1]{2,1,0:T(2,128)(2,1)}, u32[]{:S(2)}, u32[]{:S(2)}) collective-permute-start(bf16[1,1,1]{2,1,0:T(2,128)(2,1)} %bitcast.3), channel_id=1, source_target_pairs={{0,2},{1,3},{2,0},{3,1},{4,6},{5,7},{6,4},{7,5},{8,10},{9,11},{10,... | collective-permute-start | bytes 14 | tf_op jit(solution)/shard_map/ppermute | solution.py:20
  15.0 1.3 collective-permute-start.2
  16.3 0.7 slice.3
  17.0 0.2 fusion
  17.2 0.1 copy.13
  17.3 0.2 reshape.94
  17.5 0.1 broadcast_multiply_fusion
  17.6 0.7 copy.14
  18.2 4.2 %all-to-all-start = ((bf16[2,4,3200]{2,0,1:T(2,128)(2,1)}), bf16[2,4,3200]{2,0,1:T(2,128)(2,1)S(1)}, u32[]{:S(2)}, u32[]{:S(2)}) async-start(bf16[2,4,3200]{2,0,1:T(2,128)(2,1)} %copy.14), calls=%async_computation | async-start | bytes 102400 | tf_op jit(solution)/shard_map/all_to_all | solution.py:64
  22.4 0.1 dynamic_update_slice.16
  22.6 0.7 dynamic_update_slice.17
  23.3 0.7 dynamic_update_slice.18
  24.1 0.7 dynamic_update_slice.19
  24.8 0.7 convert_reduce_fusion.1
  25.6 1.7 %all-to-all-done = bf16[2,4,3200]{2,0,1:T(2,128)(2,1)S(1)} async-done(((bf16[2,4,3200]{2,0,1:T(2,128)(2,1)}), bf16[2,4,3200]{2,0,1:T(2,128)(2,1)S(1)}, u32[]{:S(2)}, u32[]{:S(2)}) %all-to-all-start) | async-done | bytes 51232 | tf_op jit(solution)/shard_map/all_to_all | solution.py:64
  27.3 0.1 reduce_sum.21
  27.5 0.3 reshape.102
  27.7 27.2 %all-reduce = (f32[32,100]{1,0:T(8,128)S(1)}, f32[]{:T(128)}) all-reduce(f32[32,100]{1,0:T(8,128)S(1)} %reduce_sum.21, f32[]{:T(128)} %convert_reduce_fusion.1), channel_id=1, replica_groups=mesh['dp'=8,'pos'=4] {'dp'}, use_global_device_ids=true, to_apply=%region_1.0 | all-reduce | flops 3201 | bytes 25608 | tf_op jit(solution)/shard_map/psum | solution.py:41
  54.9 1.9 %broadcast_multiply_fusion.1 = (f32[32,100]{1,0:T(8,128)S(1)}, f32[32,100]{1,0:T(8,128)S(1)}, f32[32,100]{1,0:T(8,128)S(1)}, f32[32,100]{1,0:T(8,128)}) fusion(f32[]{:T(128)} %convert_reduce_fusion.1, f32[32,100]{1,0:T(8,128)S(1)} %reduce_sum.21, f32[32,100]{1,0:T(8,128)S(1)} %get-tuple-element.8, f32[]{:T(128)} %get-tuple-element.9), kind=kLoop, calls=%fused_computation.15 | loop fusion | flops 12800 | bytes 76808 | tf_op jit(solution)/shard_map/mul | solution.py:44
  56.9 4.4 %multiply_add_fusion = f32[32,100,100]{2,1,0:T(8,128)} fusion(f32[32,100]{1,0:T(8,128)S(1)} %get-tuple-element.10, f32[32,100]{1,0:T(8,128)S(1)} %get-tuple-element.11, f32[8,32,100]{2,1,0:T(8,128)S(1)} %subtract_multiply_fusion), kind=kOutput, calls=%fused_computation.1 | convolution fusion | flops 31360000 | bytes 1408000 | tf_op jit(solution)/shard_map/gpc,gpd->pcd/dot_general | solution.py:36
  62.0 59.0 %all-reduce.3.cloned.1.call-done = f32[32,100,100]{2,1,0:T(8,128)} async-done(((f32[32,100,100]{2,1,0:T(8,128)}), f32[32,100,100]{2,1,0:T(8,128)}) %all-reduce.3.cloned.1.call-update) | async-done | bytes 1280016 | tf_op jit(solution)/shard_map/psum | solution.py:73
  121.0 1.6 %divide_add_fusion = f32[32,100,100]{2,1,0:T(8,128)S(1)} fusion(f32[32,100,100]{2,1,0:T(8,128)} %all-reduce.3.cloned.1.call-done, f32[100,100]{1,0:T(8,128)S(1)} %fusion.5, f32[]{:T(128)S(6)} %sub.17), kind=kLoop, calls=%fused_computation | loop fusion | flops 640000 | bytes 2600004 | tf_op jit(solution)/shard_map/add | solution.py:74
  122.6 1.5 %copy.17 = f32[32,100,100]{2,0,1:T(8,128)} copy(f32[32,100,100]{2,1,0:T(8,128)S(1)} %divide_add_fusion) | data formatting | bytes 2560000
  (16 shorter events, 0.4 us)
Async XLA Ops:
  7.2 9.8 %copy-start = (bf16[2,128,224]{1,2,0:T(8,128)(2,1)S(1)}, bf16[2,128,224]{1,2,0:T(8,128)(2,1)}, u32[]{:S(2)}) copy-start(bf16[2,128,224]{1,2,0:T(8,128)(2,1)} %param.3) | copy-start | bytes 344068
  7.9 14.7 %collective-permute-start = (bf16[1,1,1]{2,1,0:T(2,128)(2,1)}, bf16[1,1,1]{2,1,0:T(2,128)(2,1)}, u32[]{:S(2)}, u32[]{:S(2)}) collective-permute-start(bf16[1,1,1]{2,1,0:T(2,128)(2,1)} %bitcast.3), channel_id=1, source_target_pairs={{0,1},{1,0},{2,3},{3,2},{4,5},{5,4},{6,7},{7,6},{8,9},{9,8},{10,11... | collective-permute-start | bytes 14 | tf_op jit(solution)/shard_map/ppermute | solution.py:20
  12.2 11.1 %collective-permute-start.1 = (bf16[1,1,1]{2,1,0:T(2,128)(2,1)}, bf16[1,1,1]{2,1,0:T(2,128)(2,1)}, u32[]{:S(2)}, u32[]{:S(2)}) collective-permute-start(bf16[1,1,1]{2,1,0:T(2,128)(2,1)} %bitcast.3), channel_id=1, source_target_pairs={{0,2},{1,3},{2,0},{3,1},{4,6},{5,7},{6,4},{7,5},{8,10},{9,11},{10,... | collective-permute-start | bytes 14 | tf_op jit(solution)/shard_map/ppermute | solution.py:20
  15.0 9.1 %collective-permute-start.2 = (bf16[1,1,1]{2,1,0:T(2,128)(2,1)}, bf16[1,1,1]{2,1,0:T(2,128)(2,1)}, u32[]{:S(2)}, u32[]{:S(2)}) collective-permute-start(bf16[1,1,1]{2,1,0:T(2,128)(2,1)} %bitcast.3), channel_id=1, source_target_pairs={{0,3},{1,2},{2,1},{3,0},{4,7},{5,6},{6,5},{7,4},{8,11},{9,10},{10,... | collective-permute-start | bytes 14 | tf_op jit(solution)/shard_map/ppermute | solution.py:20
  18.2 9.0 %all-to-all-start = ((bf16[2,4,3200]{2,0,1:T(2,128)(2,1)}), bf16[2,4,3200]{2,0,1:T(2,128)(2,1)S(1)}, u32[]{:S(2)}, u32[]{:S(2)}) async-start(bf16[2,4,3200]{2,0,1:T(2,128)(2,1)} %copy.14), calls=%async_computation | async-start | bytes 102400 | tf_op jit(solution)/shard_map/all_to_all | solution.py:64
  22.4 98.5 %all-reduce.3.cloned.1.call-start = ((), (), s32[]{:S(2)}) async-start(), calls=%async_computation.1 | async-start | bytes 3407872 | tf_op jit(solution)/shard_map/psum | solution.py:73
Sparse Core Ops, SparseCore 0:
  61.5 59.4 all-reduce.2

commit v2 on v0

--- a/solution.py
+++ b/solution.py
@@ -1,9 +1,17 @@
+import functools
 import jax
 import jax.numpy as jnp
 from jax import lax
 from jax.sharding import PartitionSpec as P
 
 CH = 100
+
+
+def return_all_the_pools(vec, shard_axis):
+    return jnp.sum(lax.all_gather(vec, shard_axis), axis=0)
+
+
+report_stacks_all_up = functools.partial(return_all_the_pools, shard_axis="dp")
 
 
 def local_stats(received, source_counts, slots, rows, width):
@@ -54,7 +62,7 @@
     )
     total_count, mean, offset, weighted = common_mean(group_count, group_sums, group_mean)
     own_term = products + offset[:, :, None] * weighted[:, None, :]
-    summed = lax.psum(own_term, "dp")
+    summed = report_stacks_all_up(own_term)
     covariance = summed / (total_count[0] - 1.0) + 0.01 * identity
     return (mean, covariance)
 

time: 130 us -> 195 us (1.50)
  waiting for transfers between devices: 65 us -> 124 us
  other arithmetic: 4.59 us -> 10.6 us
    all_gather x0 -> x1, waiting for transfers between devices: none -> 117 us  [return_all_the_pools(): return jnp.sum(lax.all_gather(vec, shard_axis), axis=0)]
    psum x1 -> x0, waiting for transfers between devices: 58.5 us -> none  [on_device(): summed = lax.psum(own_term, 'dp')]
    reduce_sum x0 -> x1, other arithmetic: none -> 6.72 us  [return_all_the_pools(): return jnp.sum(lax.all_gather(vec, shard_axis), axis=0)]
  transfers between devices with their start and end apart: 3 -> 3, of which waited for: 3 -> 3; matrix products, arithmetic and copies ran while one was open for 2% -> 1% of each run, Pallas kernels for 0% -> 0%
where the time goes in v2:
time: 195 us
  waiting for transfers between devices  124 us (64%)
  blocking collectives  27.5 us (14%)
  between operations  15.4 us (8%)
  other arithmetic  10.6 us (5%)
  starting transfers between devices  8.48 us (4%)
  local copies, waits for them, and re-layouts  5.59 us (3%)
  matrix products  3.42 us (2%)
    all_gather x1, waiting for transfers between devices, return_all_the_pools(): return jnp.sum(lax.all_gather(vec, shard_axis), axis=0)  117 us
    psum x1, blocking collectives, common_mean(): total_count, total_sums = lax.psum((group_count, group_sums), 'dp')  27.5 us
    reduce_sum x1, other arithmetic, return_all_the_pools(): return jnp.sum(lax.all_gather(vec, shard_axis), axis=0)  6.72 us
    all_to_all x1, starting transfers between devices, on_device(): lax.all_to_all(owned_wire, 'pos', split_axis=1, concat_axis=0, tiled=True)  5.16 us
  transfers between devices with their start and end apart: 3, of which 3 were waited for; matrix products, arithmetic and copies ran while one was open for 1% of the time, Pallas kernels for 0%

profile of v2, /device:TPU:0, one launch (start us, length us, event | category | flops | bytes accessed | tf_op | source)
XLA Modules:
  0.0 194.6 jit_solution(15533061077341183164)
XLA Ops:
  7.9 0.6 broadcast_in_dim.2
  8.4 5.2 %all-to-all-start.1 = ((bf16[1,4,1]{2,0,1:T(2,128)(2,1)}), bf16[1,4,1]{2,0,1:T(2,128)(2,1)S(1)}, u32[]{:S(2)}, u32[]{:S(2)}) async-start(bf16[1,4,1]{2,0,1:T(2,128)(2,1)} %broadcast_in_dim.2), calls=%async_computation.1 | async-start | bytes 4096 | tf_op jit(solution)/shard_map/all_to_all | solution.py:57
  13.6 0.7 slice.3
  14.3 0.2 fusion.1
  14.5 0.1 copy.19
  14.6 0.2 reshape.81
  14.8 0.1 broadcast_multiply_fusion
  14.9 0.7 copy.20
  15.6 2.6 %all-to-all-done.1 = bf16[1,4,1]{2,0,1:T(2,128)(2,1)S(1)} async-done(((bf16[1,4,1]{2,0,1:T(2,128)(2,1)}), bf16[1,4,1]{2,0,1:T(2,128)(2,1)S(1)}, u32[]{:S(2)}, u32[]{:S(2)}) %all-to-all-start.1) | async-done | bytes 40 | tf_op jit(solution)/shard_map/all_to_all | solution.py:57
  18.2 3.3 %all-to-all-start = ((bf16[2,4,3200]{2,0,1:T(2,128)(2,1)}), bf16[2,4,3200]{2,0,1:T(2,128)(2,1)S(1)}, u32[]{:S(2)}, u32[]{:S(2)}) async-start(bf16[2,4,3200]{2,0,1:T(2,128)(2,1)} %copy.20), calls=%async_computation | async-start | bytes 102400 | tf_op jit(solution)/shard_map/all_to_all | solution.py:56
  21.5 0.7 convert_reduce_fusion.1
  22.3 0.1 reshape.85
  22.4 3.9 %all-to-all-done = bf16[2,4,3200]{2,0,1:T(2,128)(2,1)S(1)} async-done(((bf16[2,4,3200]{2,0,1:T(2,128)(2,1)}), bf16[2,4,3200]{2,0,1:T(2,128)(2,1)S(1)}, u32[]{:S(2)}, u32[]{:S(2)}) %all-to-all-start) | async-done | bytes 51232 | tf_op jit(solution)/shard_map/all_to_all | solution.py:56
  26.3 0.1 reduce_sum.30
  26.5 0.3 reshape.84
  26.7 27.5 %all-reduce = (f32[32,100]{1,0:T(8,128)S(1)}, f32[]{:T(128)}) all-reduce(f32[32,100]{1,0:T(8,128)S(1)} %reduce_sum.30, f32[]{:T(128)} %get-tuple-element.7), channel_id=1, replica_groups=mesh['dp'=8,'pos'=4] {'dp'}, use_global_device_ids=true, to_apply=%region_1.0 | all-reduce | flops 3201 | bytes 25608 | tf_op jit(solution)/shard_map/psum | solution.py:33
  54.2 1.9 broadcast_multiply_fusion.1
  56.1 0.1 subtract_multiply_fusion
  56.2 3.2 %multiply_add_fusion = f32[32,100,100]{2,1,0:T(8,128)S(1)} fusion(f32[32,100]{1,0:T(8,128)S(1)} %get-tuple-element.10, f32[32,100]{1,0:T(8,128)S(1)} %get-tuple-element.11, f32[8,32,100]{2,1,0:T(8,128)S(1)} %subtract_multiply_fusion), kind=kOutput, calls=%fused_computation.2 | convolution fusion | flops 31360000 | bytes 1408000 | tf_op jit(solution)/shard_map/gpc,gpd->pcd/dot_general | solution.py:28
  59.4 1.5 copy.23
  61.5 117.0 %all-gather.3.cloned.1.call-done = f32[256,100,100]{2,0,1:T(8,128)} async-done(((f32[32,100,100]{2,0,1:T(8,128)}), f32[256,100,100]{2,0,1:T(8,128)}) %all-gather.3.cloned.1.call-update) | async-done | bytes 10240016 | tf_op jit(solution)/shard_map/all_gather | solution.py:11
  178.6 6.7 %reduce_sum.32 = f32[32,100,100]{2,0,1:T(8,128)S(1)} reduce(f32[8,32,100,100]{3,1,0,2:T(8,128)} %bitcast.19, f32[]{:T(128)} %constant.2.clone.1), dimensions={0}, to_apply=%region_4.0 | reduce | flops 2240000 | bytes 11520004 | tf_op jit(solution)/shard_map/reduce_sum | solution.py:11
  185.3 1.0 fusion
  186.3 1.5 copy.25
  (9 shorter events, 0.3 us)
Async XLA Ops:
  7.2 7.1 %copy-start = (bf16[2,128,224]{1,2,0:T(8,128)(2,1)S(1)}, bf16[2,128,224]{1,2,0:T(8,128)(2,1)}, u32[]{:S(2)}) copy-start(bf16[2,128,224]{1,2,0:T(8,128)(2,1)} %param.3) | copy-start | bytes 344068
  8.4 9.7 %all-to-all-start.1 = ((bf16[1,4,1]{2,0,1:T(2,128)(2,1)}), bf16[1,4,1]{2,0,1:T(2,128)(2,1)S(1)}, u32[]{:S(2)}, u32[]{:S(2)}) async-start(bf16[1,4,1]{2,0,1:T(2,128)(2,1)} %broadcast_in_dim.2), calls=%async_computation.1 | async-start | bytes 4096 | tf_op jit(solution)/shard_map/all_to_all | solution.py:57
  18.2 8.1 %all-to-all-start = ((bf16[2,4,3200]{2,0,1:T(2,128)(2,1)}), bf16[2,4,3200]{2,0,1:T(2,128)(2,1)S(1)}, u32[]{:S(2)}, u32[]{:S(2)}) async-start(bf16[2,4,3200]{2,0,1:T(2,128)(2,1)} %copy.20), calls=%async_computation | async-start | bytes 102400 | tf_op jit(solution)/shard_map/all_to_all | solution.py:56
  21.5 157.1 %all-gather.3.cloned.1.call-start = ((), (), s32[]{:S(2)}) async-start(), calls=%async_computation.2 | async-start | bytes 14745600 | tf_op jit(solution)/shard_map/all_gather | solution.py:11
Sparse Core Ops, SparseCore 0:
  61.0 117.4 all-gather.2
